TPU v7x, 128 devices: a whole 4x4x4 slice. The times are simulated.
128 devices in a mesh: tok: 8 (over z, core), lat: 16 (over y, x).
Axes of the slice: x: 4, y: 4, z: 4, core: 2. Of those that a mesh axis runs over, the one named last changes fastest.
Arguments:
- activations: bfloat16 [2048, 2, 8192], P('lat', None, 'tok'), may hold values from -6 to 6
- enc_weight: bfloat16 [64, 2, 8192, 256], P('lat', None, 'tok'), may hold values from -0.046875 to 0.046875
- enc_bias: float32 [64, 256], P('lat'), may hold values from -3 to 3
- dec_weight: bfloat16 [64, 256, 2, 8192], P('lat', None, None, 'tok'), may hold values from -0.09375 to 0.09375
- dec_bias: float32 [2, 8192], P(None, 'tok'), may hold values from -3 to 3
- active: int32 [16, 16], replicated, may hold values from 0 to 63, all different within a row; in each aligned block of 16 rows (0 to 15, 16 to 31, ...) at most 8 rows name the same one
Outputs:
- grad_enc: bfloat16 [64, 2, 8192, 256], P('lat', None, 'tok')
- grad_enc_bias: float32 [64, 256], P('lat')
- grad_dec: bfloat16 [64, 256, 2, 8192], P('lat', None, None, 'tok')
- grad_dec_bias: float32 [2, 8192], P(None, 'tok')
Inputs may be any that keep to these rules, and one draw needn't show every extreme that they name: `active`: each row lists 16 different block ids; every block id appears in some row; no block id appears in more than 8 rows, and some block id appears in exactly 8 rows.
All inputs are finite; a program needn't handle non-finite values.
Results may differ from a plain program's by a relative error of at most 0.02.
Values may be sent and summed in bfloat16 or wider, within the bound.
A program may use at most 192 MiB of HBM per device.

v0:
```python
import math
import jax
import jax.numpy as jnp
from jax import lax
from jax.sharding import PartitionSpec as P

MOST = 8
TILE = 128
SPARSITY = 0.25
NORM_EPSILON = 1e-06


def slot_lists(active, first_block, block_count):
    tile_count = active.shape[0]
    block_ids = first_block + jnp.arange(block_count, dtype=jnp.int32)
    is_active = jnp.any(active[:, :, None] == block_ids[None, None, :], axis=1).astype(jnp.int32)
    rank_count = jnp.cumsum(is_active, axis=0)
    wanted = jnp.arange(MOST, dtype=jnp.int32) + 1
    picked = (is_active[:, :, None] == 1) & (rank_count[:, :, None] == wanted[None, None, :])
    tile_ids = jnp.arange(tile_count, dtype=jnp.int32)
    slot_tile = jnp.sum(jnp.where(picked, tile_ids[:, None, None], 0), axis=0)
    live_slot = jnp.any(picked, axis=0)
    return (slot_tile, live_slot)


def on_device(activations, enc_weight, enc_bias, dec_weight, dec_bias, active):
    slab_count = enc_weight.shape[0]
    tile_count = active.shape[0]
    tile_rows = activations.shape[0]
    models = activations.shape[1]
    feat_width = activations.shape[2]
    loss_scale = 1.0 / math.sqrt(MOST * TILE)
    first_block = lax.axis_index("lat") * slab_count
    slot_tile, live_slot = slot_lists(active, first_block, slab_count)
    live_mask = live_slot[:, :, None, None]
    gathered = lax.all_gather(activations, "lat", axis=0, tiled=True)
    tile_acts = gathered.reshape(tile_count, tile_rows, models, feat_width)
    chosen = tile_acts[slot_tile]
    pre_part = jnp.einsum(
        "smrad,sadj->smrj", chosen, enc_weight, preferred_element_type=jnp.float32
    )
    pre_act = lax.psum(pre_part, "tok") + enc_bias[:, None, None, :]
    features = jnp.where(live_mask, jnp.maximum(pre_act, 0.0), 0.0).astype(jnp.bfloat16)
    product = jnp.einsum(
        "smrj,sjad->smrad", features, dec_weight, preferred_element_type=jnp.float32
    )
    partial_value = (
        jnp.zeros((tile_count, tile_rows, models, feat_width), jnp.float32)
        .at[slot_tile]
        .add(product)
    )
    rounded = lax.optimization_barrier(partial_value.astype(jnp.bfloat16)).astype(jnp.float32)
    rounded = rounded.reshape(tile_count * tile_rows, models, feat_width)
    recon_mine = (
        lax.psum_scatter(
            rounded.astype(jnp.bfloat16), "lat", scatter_dimension=0, tiled=True
        ).astype(jnp.float32)
        + dec_bias[None, :, :]
    )
    error_mine = (recon_mine - activations.astype(jnp.float32)).astype(jnp.bfloat16)
    error_all = lax.all_gather(error_mine, "lat", axis=0, tiled=True)
    tile_err = error_all.reshape(tile_count, tile_rows, models, feat_width)
    err_chosen = tile_err[slot_tile]
    grad_part = jnp.einsum(
        "smrad,sjad->smrj", err_chosen, dec_weight, preferred_element_type=jnp.float32
    )
    dec_wide = dec_weight.astype(jnp.float32)
    squares = jnp.sum(jnp.square(dec_wide), axis=3)
    grad_sum, square_sum = (
        lax.psum(grad_part.astype(jnp.bfloat16), "tok").astype(jnp.float32),
        lax.psum(squares.astype(jnp.bfloat16), "tok").astype(jnp.float32),
    )
    dec_norms = jnp.sqrt(square_sum + NORM_EPSILON)
    feat_grad = loss_scale * (grad_sum + SPARSITY * jnp.sum(dec_norms, axis=2)[:, None, None, :])
    pre_grad = jnp.where(features > 0, feat_grad, 0.0).astype(jnp.bfloat16)
    grad_enc = jnp.einsum(
        "smrad,smrj->sadj", chosen, pre_grad, preferred_element_type=jnp.float32
    ).astype(jnp.bfloat16)
    grad_enc_bias = jnp.sum(pre_grad.astype(jnp.float32), axis=(1, 2))
    feat_total = jnp.sum(features.astype(jnp.float32), axis=(1, 2))
    recon_term = jnp.einsum(
        "smrj,smrad->sjad", features, err_chosen, preferred_element_type=jnp.float32
    )
    norm_term = SPARSITY * feat_total[:, :, None, None] * dec_wide / dec_norms[:, :, :, None]
    grad_dec = (loss_scale * (recon_term + norm_term)).astype(jnp.bfloat16)
    grad_dec_bias = loss_scale * jnp.sum(error_all.astype(jnp.float32), axis=0)
    return (grad_enc, grad_enc_bias, grad_dec, grad_dec_bias)


def solution(mesh):
    placed = (
        P("lat", None, "tok"),
        P("lat", None, "tok", None),
        P("lat", None),
        P("lat", None, None, "tok"),
        P(None, "tok"),
        P(),
    )
    return jax.shard_map(
        on_device,
        mesh=mesh,
        in_specs=placed,
        out_specs=(
            P("lat", None, "tok", None),
            P("lat", None),
            P("lat", None, None, "tok"),
            P(None, "tok"),
        ),
        check_vma=False,
    )
```

profile of v0, /device:TPU:0, one launch (start us, length us, event | category | flops | bytes accessed | tf_op | source)
XLA Modules:
  0.0 585.7 jit_solution(5982257089558291725)
XLA Ops:
  7.2 0.0 all-gather.3.cloned.1.call-start
  7.2 2.0 copy.46
  9.2 0.0 all-gather.3.cloned.1.call-update
  9.2 0.0 all-reduce.3.cloned.1.call-start
  9.3 0.9 compare_reduce_fusion
  10.2 0.1 copy.47
  10.3 0.1 copy.48
  10.4 0.2 select_reduce_fusion
  10.6 0.1 reshape.64
  10.7 73.1 %all-gather.3.cloned.1.call-done = bf16[2048,2,1024]{2,0,1:T(8,128)(2,1)} async-done(((bf16[128,2,1024]{2,0,1:T(8,128)(2,1)}), bf16[2048,2,1024]{2,0,1:T(8,128)(2,1)}) %all-gather.3.cloned.1.call-update) | async-done | bytes 8388624 | tf_op jit(solution)/shard_map/all_gather | solution.py:36
  83.8 8.2 %copy.49 = bf16[16,128,2,1024]{3,1,2,0:T(8,128)(2,1)} copy(bf16[16,128,2,1024]{3,1,0,2:T(8,128)(2,1)} %bitcast.69) | data formatting | bytes 16777216 | tf_op jit(solution)/shard_map/reshape | solution.py:37
  92.0 10.6 %gather_fusion = bf16[32,128,2,1024]{3,1,2,0:T(8,128)(2,1)} fusion(bf16[16,128,2,1024]{3,1,2,0:T(8,128)(2,1)} %copy.49, s32[1024]{0:T(1024)S(1)} %pad_clamp_fusion), kind=kCustom, calls=%fused_computation | custom fusion | bytes 33554560 | tf_op jit(solution)/shard_map/gather | solution.py:38
  102.6 13.5 %fusion.11 = f32[4,8,128,256]{3,2,1,0:T(8,128)} fusion(bf16[4,8,128,2,1024]{4,2,3,1,0:T(8,128)(2,1)} %bitcast.65, bf16[4,2,1024,256]{3,2,1,0:T(8,128)(2,1)} %param.7), kind=kOutput, calls=%fused_computation.23 | convolution fusion | flops 4294967296 | bytes 25165824 | tf_op jit(solution)/shard_map/smrad,sadj->smrj/dot_general | solution.py:39
  116.1 0.0 copy-start.4
  116.1 0.0 all-reduce.3.cloned.1.call-update
  116.1 0.2 reduce-scatter.2.cloned.1.call-start
  116.4 0.2 fusion.19
  116.6 72.3 %all-reduce.3.cloned.1.call-done = f32[4,8,128,256]{3,2,1,0:T(8,128)} async-done(((f32[4,8,128,256]{3,2,1,0:T(8,128)}), f32[4,8,128,256]{3,2,1,0:T(8,128)}) %all-reduce.3.cloned.1.call-update) | async-done | bytes 4194320 | tf_op jit(solution)/shard_map/psum | solution.py:42
  188.9 0.0 copy-done.4
  188.9 0.0 copy-start
  188.9 3.1 select_convert_fusion.1
  192.0 0.4 copy-done
  192.3 13.1 %fusion.9 = f32[4,8,128,2,1024]{4,2,3,1,0:T(8,128)} fusion(bf16[4,256,2,1024,1]{3,2,1,0,4:T(2,128)(2,1)S(1)} %bitcast.64, bf16[4,8,128,256]{3,2,1,0:T(8,128)(2,1)S(1)} %select_convert_fusion.1), kind=kOutput, calls=%fused_computation.21 | convolution fusion | flops 4294967296 | bytes 39845888 | tf_op jit(solution)/shard_map/smrj,sjad->smrad/dot_general | solution.py:44
  205.4 7.8 %broadcast_in_dim.28 = f32[16,128,2,1024]{3,1,2,0:T(8,128)} broadcast(f32[]{:T(128)} %constant.17.clone.1), dimensions={} | broadcast | bytes 16777220 | tf_op jit(solution)/shard_map/broadcast_in_dim | solution.py:48
  213.3 65.6 %scatter_fusion = f32[16,128,2,1024]{3,1,2,0:T(8,128)} fusion(f32[16,128,2,1024]{3,1,2,0:T(8,128)} %broadcast_in_dim.28, s32[32]{0:T(128)S(1)} %reshape.64, f32[32,128,2,1024]{3,1,2,0:T(8,128)} %bitcast.60), kind=kCustom, calls=%fused_computation.2 | custom fusion | flops 8388608 | bytes 100663424 | tf_op jit(solution)/shard_map/scatter-add | solution.py:50
  278.9 9.1 %convert_element_type.66 = bf16[16,128,2,1024]{3,1,2,0:T(8,128)(2,1)} convert(f32[16,128,2,1024]{3,1,2,0:T(8,128)} %scatter_fusion) | non-fusion elementwise | flops 4194304 | bytes 25165824 | tf_op jit(solution)/shard_map/convert_element_type | solution.py:52
  288.0 8.2 %copy.51 = bf16[16,128,2,1024]{3,1,0,2:T(8,128)(2,1)} copy(bf16[16,128,2,1024]{3,1,2,0:T(8,128)(2,1)} %convert_element_type.66) | data formatting | bytes 16777216 | tf_op jit(solution)/shard_map/optimization_barrier | solution.py:52
  296.2 0.0 copy-start.3
  296.2 0.0 copy-start.5
  296.2 0.0 reduce-scatter.2.cloned.1.call-update
  296.2 0.0 all-gather.5.cloned.1.call-start
  296.2 84.8 %reduce-scatter.2.cloned.1.call-done = bf16[128,2,1024]{2,0,1:T(8,128)(2,1)} async-done(((bf16[2048,2,1024]{2,0,1:T(8,128)(2,1)}), bf16[128,2,1024]{2,0,1:T(8,128)(2,1)}) %reduce-scatter.2.cloned.1.call-update) | async-done | bytes 524304 | tf_op jit(solution)/shard_map/reduce_scatter | solution.py:55
  381.1 0.0 copy-done.3
  381.1 0.0 copy-done.5
  381.1 2.1 subtract_convert_fusion
  383.1 0.0 all-gather.5.cloned.1.call-update
  383.2 0.0 all-reduce.5.cloned.1.call-start
  383.2 3.4 fusion
  386.6 13.9 %psum.23 = bf16[4,256,2]{1,2,0:T(2,128)(2,1)S(1)} all-reduce(bf16[4,256,2]{1,2,0:T(2,128)(2,1)S(1)} %fusion), channel_id=1, replica_groups=mesh['tok'=8,'lat'=16] {'tok'}, use_global_device_ids=true, to_apply=%region_9.10 | all-reduce | flops 2048 | bytes 8192 | tf_op jit(solution)/shard_map/psum | solution.py:71
  400.5 53.2 %all-gather.5.cloned.1.call-done = bf16[2048,2,1024]{2,0,1:T(8,128)(2,1)} async-done(((bf16[128,2,1024]{2,0,1:T(8,128)(2,1)}), bf16[2048,2,1024]{2,0,1:T(8,128)(2,1)}) %all-gather.5.cloned.1.call-update) | async-done | bytes 8388624 | tf_op jit(solution)/shard_map/all_gather | solution.py:61
  453.7 10.6 %gather_fusion.1 = bf16[32,128,2,1024]{3,1,2,0:T(8,128)(2,1)} fusion(bf16[16,128,2,1024]{3,1,0,2:T(8,128)(2,1)} %bitcast.61, s32[1024]{0:T(1024)S(1)} %pad_clamp_fusion), kind=kCustom, calls=%fused_computation.1 | custom fusion | bytes 33554560 | tf_op jit(solution)/shard_map/gather | solution.py:63
  464.4 12.8 %bitcast_convert_fusion.1 = bf16[4,8,128,256]{3,2,1,0:T(8,128)(2,1)} fusion(bf16[4,8,128,2,1024]{4,2,3,1,0:T(8,128)(2,1)} %bitcast.67, bf16[4,256,2,1024,1]{3,2,1,0,4:T(2,128)(2,1)} %bitcast.63), kind=kOutput, calls=%fused_computation.14 | convolution fusion | flops 4296015872 | bytes 23068672 | tf_op jit(solution)/shard_map/smrad,sjad->smrj/dot_general | solution.py:64
  477.2 0.0 all-reduce.5.cloned.1.call-update
  477.3 5.0 convert_reduce_fusion
  482.3 0.6 broadcast_multiply_fusion
  482.9 60.1 %all-reduce.5.cloned.1.call-done = bf16[4,8,128,256]{3,2,1,0:T(8,128)(2,1)} async-done(((bf16[4,8,128,256]{3,2,1,0:T(8,128)(2,1)}), bf16[4,8,128,256]{3,2,1,0:T(8,128)(2,1)}) %all-reduce.5.cloned.1.call-update) | async-done | bytes 2097168 | tf_op jit(solution)/shard_map/psum | solution.py:70
  543.0 0.0 copy-start.1
  543.0 5.1 convert_reduce_fusion.1
  548.0 0.0 copy-done.1
  548.0 10.7 %fusion.4 = bf16[4,256,2,1024]{3,1,2,0:T(8,128)(2,1)} fusion(f32[4,256,2]{1,2,0:T(2,128)S(1)} %get-tuple-element.26, f32[4,256]{1,0:T(4,128)S(1)} %broadcast_multiply_fusion.1, bf16[4,256,2,1024]{3,2,1,0:T(2,128)(2,1)S(1)} %copy-done.1, bf16[4,8,128,2,1024]{4,2,3,1,0:T(8,128)(2,1)} %bitcast.68, bf16[4,8,128,256]{3,2,1,0:T(8,128)(2,1)S(1)} %select_convert_fusion.1), kind=kOutput, calls=%fused_computation.11 | convolution fusion | flops 4307550208 | bytes 27275264 | tf_op jit(solution)/shard_map/smrj,smrad->sjad/dot_general | solution.py:81
  558.7 0.0 copy-start.2
  558.7 8.7 %copy.58 = bf16[4,256,2,1024]{3,2,1,0:T(2,128)(2,1)} copy(bf16[4,256,2,1024]{3,1,2,0:T(8,128)(2,1)} %fusion.4) | data formatting | bytes 8388608
  567.4 0.0 copy-done.2
  567.4 11.8 %bitcast_convert_fusion = bf16[4,2,1024,256]{3,2,1,0:T(8,128)(2,1)} fusion(bf16[4,8,128,2,1024]{4,2,3,1,0:T(8,128)(2,1)} %bitcast.66, bf16[4,8,128,256]{3,2,1,0:T(8,128)(2,1)S(1)} %copy-done.2, bf16[4,8,128,256]{3,2,1,0:T(8,128)(2,1)S(1)} %select_convert_fusion.1, f32[4,256]{1,0:T(4,128)S(1)} %broadcast_multiply_fusion.2), kind=kOutput, calls=%fused_computation.10 | convolution fusion | flops 4303355904 | bytes 25169920 | tf_op jit(solution)/shard_map/smrad,smrj->sadj/dot_general | solution.py:76
  (9 shorter events, 0.1 us)
Async XLA Ops:
  7.2 76.7 %all-gather.3.cloned.1.call-start = ((), (), s32[]{:S(2)}) async-start(), calls=%async_computation.1 | async-start | bytes 8912896 | tf_op jit(solution)/shard_map/all_gather | solution.py:36
  9.2 179.7 %all-reduce.3.cloned.1.call-start = ((), (), s32[]{:S(2)}) async-start(), calls=%async_computation.2 | async-start | bytes 8388608 | tf_op jit(solution)/shard_map/psum | solution.py:42
  116.1 72.8 %copy-start.4 = (f32[4,256]{1,0:T(4,128)S(1)}, f32[4,256]{1,0:T(4,128)}, u32[]{:S(2)}) copy-start(f32[4,256]{1,0:T(4,128)} %param.8) | copy-start | bytes 12292
  116.1 265.0 %reduce-scatter.2.cloned.1.call-start = ((), (), s32[]{:S(2)}) async-start(), calls=%async_computation.3 | async-start | bytes 8912896 | tf_op jit(solution)/shard_map/reduce_scatter | solution.py:55
  188.9 3.4 copy-start
  296.2 84.9 %copy-start.3 = (bf16[128,2,1024]{2,1,0:T(2,128)(2,1)S(1)}, bf16[128,2,1024]{2,1,0:T(2,128)(2,1)}, u32[]{:S(2)}) copy-start(bf16[128,2,1024]{2,1,0:T(2,128)(2,1)} %param.6) | copy-start | bytes 1572868
  296.2 84.9 %copy-start.5 = (f32[2,1024]{1,0:T(2,128)S(1)}, f32[2,1024]{1,0:T(2,128)}, u32[]{:S(2)}) copy-start(f32[2,1024]{1,0:T(2,128)} %param.10) | copy-start | bytes 24580
  296.2 157.5 %all-gather.5.cloned.1.call-start = ((), (), s32[]{:S(2)}) async-start(), calls=%async_computation.4 | async-start | bytes 8912896 | tf_op jit(solution)/shard_map/all_gather | solution.py:61
  383.2 159.8 %all-reduce.5.cloned.1.call-start = ((), (), s32[]{:S(2)}) async-start(), calls=%async_computation.5 | async-start | bytes 4194304 | tf_op jit(solution)/shard_map/psum | solution.py:70
  543.0 5.1 copy-start.1
  558.7 8.7 %copy-start.2 = (bf16[4,8,128,256]{3,2,1,0:T(8,128)(2,1)S(1)}, bf16[4,8,128,256]{3,2,1,0:T(8,128)(2,1)}, u32[]{:S(2)}) copy-start(bf16[4,8,128,256]{3,2,1,0:T(8,128)(2,1)} %all-reduce.5.cloned.1.call-done) | copy-start | bytes 6291460
Sparse Core Ops, SparseCore 0:
  10.7 73.0 all-gather.2
  116.2 72.5 all-reduce.2
  296.3 84.7 reduce-scatter.1
  383.7 70.0 all-gather.4
  477.3 65.6 all-reduce.4
where the time goes:
time: 586 us
  waiting for transfers between devices  344 us (59%)
  other arithmetic  95.3 us (16%)
  matrix products  61.8 us (11%)
  local copies, waits for them, and re-layouts  56.7 us (10%)
  blocking collectives  13.9 us (2%)
  between operations  13.8 us (2%)
    reduce_scatter x1, waiting for transfers between devices, on_device(): lax.psum_scatter(rounded.astype(jnp.bfloat16), 'lat', scatter_dimension=0...  84.8 us
    all_gather x1, waiting for transfers between devices, on_device(): gathered = lax.all_gather(activations, 'lat', axis=0, tiled=True)  73.1 us
    psum x1, waiting for transfers between devices, on_device(): pre_act = lax.psum(pre_part, 'tok') + enc_bias[:, None, None, :]  72.3 us
    scatter-add x1, other arithmetic, on_device(): partial_value = jnp.zeros((tile_count, tile_rows, models, feat_width), jn...  65.6 us
    psum x1, waiting for transfers between devices, on_device(): lax.psum(grad_part.astype(jnp.bfloat16), 'tok').astype(jnp.float32)  60.1 us
    all_gather x1, waiting for transfers between devices, on_device(): error_all = lax.all_gather(error_mine, 'lat', axis=0, tiled=True)  53.2 us
    psum x1, blocking collectives, on_device(): lax.psum(squares.astype(jnp.bfloat16), 'tok').astype(jnp.float32)  13.9 us
    dot_general x1, matrix products, on_device(): jnp.einsum('smrad,sadj->smrj', chosen, enc_weight, preferred_element_type...  13.5 us
  transfers between devices with their start and end apart: 5, of which 5 were waited for; matrix products, arithmetic and copies ran while one was open for 2% of the time, Pallas kernels for 0%

commit v1 on v0

--- a/solution.py
+++ b/solution.py
@@ -33,7 +33,9 @@
     first_block = lax.axis_index("lat") * slab_count
     slot_tile, live_slot = slot_lists(active, first_block, slab_count)
     live_mask = live_slot[:, :, None, None]
-    gathered = lax.all_gather(activations, "lat", axis=0, tiled=True)
+    gathered = jnp.concatenate(
+        lax.all_to_all(jnp.stack([activations] * lax.axis_size("lat")), "lat", 0, 0), axis=0
+    )
     tile_acts = gathered.reshape(tile_count, tile_rows, models, feat_width)
     chosen = tile_acts[slot_tile]
     pre_part = jnp.einsum(

time: 586 us -> 639 us (1.090)
  waiting for transfers between devices: 344 us -> 395 us
  starting transfers between devices: 0.39 us -> 7.65 us
    all_to_all x0 -> x1, waiting for transfers between devices: none -> 123 us  [on_device(): lax.all_to_all(jnp.stack([activations] * lax.axis_size('lat')), 'lat', 0, 0)]
    all_gather x1 -> x0, waiting for transfers between devices: 73.1 us -> none  [on_device(): gathered = lax.all_gather(activations, 'lat', axis=0, tiled=True)]
    reshape x1 -> x0, local copies, waits for them, and re-layouts: 8.19 us -> none  [on_device(): tile_acts = gathered.reshape(tile_count, tile_rows, models, feat_width)]
    all_to_all x0 -> x1, starting transfers between devices: none -> 7.3 us  [on_device(): lax.all_to_all(jnp.stack([activations] * lax.axis_size('lat')), 'lat', 0, 0)]
where the time goes in v1:
time: 639 us
  waiting for transfers between devices  395 us (62%)
  other arithmetic  94.6 us (15%)
  matrix products  61.8 us (10%)
  local copies, waits for them, and re-layouts  52 us (8%)
  between operations  13.9 us (2%)
  blocking collectives  13.8 us (2%)
  starting transfers between devices  7.65 us (1%)
    all_to_all x1, waiting for transfers between devices, on_device(): lax.all_to_all(jnp.stack([activations] * lax.axis_size('lat')), 'lat', 0, 0)  123 us
    reduce_scatter x1, waiting for transfers between devices, on_device(): lax.psum_scatter(rounded.astype(jnp.bfloat16), 'lat', scatter_dimension=0...  84.7 us
    psum x1, waiting for transfers between devices, on_device(): pre_act = lax.psum(pre_part, 'tok') + enc_bias[:, None, None, :]  73.6 us
    scatter-add x1, other arithmetic, on_device(): partial_value = jnp.zeros((tile_count, tile_rows, models, feat_width), jn...  65.6 us
    psum x1, waiting for transfers between devices, on_device(): lax.psum(grad_part.astype(jnp.bfloat16), 'tok').astype(jnp.float32)  60.1 us
    all_gather x1, waiting for transfers between devices, on_device(): error_all = lax.all_gather(error_mine, 'lat', axis=0, tiled=True)  53.5 us
    psum x1, blocking collectives, on_device(): lax.psum(squares.astype(jnp.bfloat16), 'tok').astype(jnp.float32)  13.8 us
    dot_general x1, matrix products, on_device(): jnp.einsum('smrad,sadj->smrj', chosen, enc_weight, preferred_element_type...  13.5 us
  transfers between devices with their start and end apart: 5, of which 5 were waited for; matrix products, arithmetic and copies ran while one was open for 2% of the time, Pallas kernels for 0%

profile of v1, /device:TPU:0, one launch (start us, length us, event | category | flops | bytes accessed | tf_op | source)
XLA Modules:
  0.0 638.9 jit_solution(12155435040882415463)
XLA Ops:
  7.2 1.2 copy.36
  8.3 4.3 stack.2
  12.6 0.0 copy-start.6
  12.6 7.3 %all-to-all-start = ((bf16[16,128,2,1024]{3,1,2,0:T(8,128)(2,1)}), bf16[16,128,2,1024]{3,1,2,0:T(8,128)(2,1)}, u32[]{:S(2)}, u32[]{:S(2)}) async-start(bf16[16,128,2,1024]{3,1,2,0:T(8,128)(2,1)} %stack.2), calls=%async_computation | async-start | bytes 16777216 | tf_op jit(solution)/shard_map/all_to_all | solution.py:37
  19.9 0.0 all-reduce.3.cloned.1.call-start
  20.0 0.0 copy-done.6
  20.0 0.2 compare_reduce_fusion
  20.3 0.1 copy.37
  20.4 0.1 copy.38
  20.5 0.2 select_reduce_fusion
  20.7 0.1 reshape.62
  20.8 123.2 %all-to-all-done = bf16[16,128,2,1024]{3,1,2,0:T(8,128)(2,1)} async-done(((bf16[16,128,2,1024]{3,1,2,0:T(8,128)(2,1)}), bf16[16,128,2,1024]{3,1,2,0:T(8,128)(2,1)}, u32[]{:S(2)}, u32[]{:S(2)}) %all-to-all-start) | async-done | bytes 8388640 | tf_op jit(solution)/shard_map/all_to_all | solution.py:37
  144.0 10.6 %gather_fusion = bf16[32,128,2,1024]{3,1,2,0:T(8,128)(2,1)} fusion(bf16[16,128,2,1024]{3,1,2,0:T(8,128)(2,1)} %all-to-all-done, s32[1024]{0:T(1024)S(1)} %pad_clamp_fusion), kind=kCustom, calls=%fused_computation | custom fusion | bytes 33554560 | tf_op jit(solution)/shard_map/gather | solution.py:40
  154.6 13.5 %fusion.11 = f32[4,8,128,256]{3,2,1,0:T(8,128)} fusion(bf16[4,8,128,2,1024]{4,2,3,1,0:T(8,128)(2,1)} %bitcast.64, bf16[4,2,1024,256]{3,2,1,0:T(8,128)(2,1)} %param.7), kind=kOutput, calls=%fused_computation.23 | convolution fusion | flops 4294967296 | bytes 25165824 | tf_op jit(solution)/shard_map/smrad,sadj->smrj/dot_general | solution.py:41
  168.0 0.0 copy-start.4
  168.0 0.0 all-reduce.3.cloned.1.call-update
  168.1 0.2 reduce-scatter.2.cloned.1.call-start
  168.3 0.2 fusion.19
  168.5 73.6 %all-reduce.3.cloned.1.call-done = f32[4,8,128,256]{3,2,1,0:T(8,128)} async-done(((f32[4,8,128,256]{3,2,1,0:T(8,128)}), f32[4,8,128,256]{3,2,1,0:T(8,128)}) %all-reduce.3.cloned.1.call-update) | async-done | bytes 4194320 | tf_op jit(solution)/shard_map/psum | solution.py:44
  242.1 0.0 copy-done.4
  242.1 0.0 copy-start
  242.1 3.1 select_convert_fusion.1
  245.2 0.4 copy-done
  245.5 13.1 %fusion.9 = f32[4,8,128,2,1024]{4,2,3,1,0:T(8,128)} fusion(bf16[4,256,2,1024,1]{3,2,1,0,4:T(2,128)(2,1)S(1)} %bitcast.63, bf16[4,8,128,256]{3,2,1,0:T(8,128)(2,1)S(1)} %select_convert_fusion.1), kind=kOutput, calls=%fused_computation.21 | convolution fusion | flops 4294967296 | bytes 39845888 | tf_op jit(solution)/shard_map/smrj,sjad->smrad/dot_general | solution.py:46
  258.6 7.8 %broadcast_in_dim.28 = f32[16,128,2,1024]{3,1,2,0:T(8,128)} broadcast(f32[]{:T(128)} %constant.17.clone.1), dimensions={} | broadcast | bytes 16777220 | tf_op jit(solution)/shard_map/broadcast_in_dim | solution.py:50
  266.5 65.6 %scatter_fusion = f32[16,128,2,1024]{3,1,2,0:T(8,128)} fusion(f32[16,128,2,1024]{3,1,2,0:T(8,128)} %broadcast_in_dim.28, s32[32]{0:T(128)S(1)} %reshape.62, f32[32,128,2,1024]{3,1,2,0:T(8,128)} %bitcast.59), kind=kCustom, calls=%fused_computation.2 | custom fusion | flops 8388608 | bytes 100663424 | tf_op jit(solution)/shard_map/scatter-add | solution.py:52
  332.1 9.1 %convert_element_type.66 = bf16[16,128,2,1024]{3,1,2,0:T(8,128)(2,1)} convert(f32[16,128,2,1024]{3,1,2,0:T(8,128)} %scatter_fusion) | non-fusion elementwise | flops 4194304 | bytes 25165824 | tf_op jit(solution)/shard_map/convert_element_type | solution.py:54
  341.2 8.2 %copy.40 = bf16[16,128,2,1024]{3,1,0,2:T(8,128)(2,1)} copy(bf16[16,128,2,1024]{3,1,2,0:T(8,128)(2,1)} %convert_element_type.66) | data formatting | bytes 16777216 | tf_op jit(solution)/shard_map/optimization_barrier | solution.py:54
  349.4 0.0 copy-start.3
  349.4 0.0 copy-start.5
  349.4 0.0 reduce-scatter.2.cloned.1.call-update
  349.4 0.0 all-gather.2.cloned.1.call-start
  349.5 84.7 %reduce-scatter.2.cloned.1.call-done = bf16[128,2,1024]{2,0,1:T(8,128)(2,1)} async-done(((bf16[2048,2,1024]{2,0,1:T(8,128)(2,1)}), bf16[128,2,1024]{2,0,1:T(8,128)(2,1)}) %reduce-scatter.2.cloned.1.call-update) | async-done | bytes 524304 | tf_op jit(solution)/shard_map/reduce_scatter | solution.py:57
  434.1 0.0 copy-done.3
  434.1 0.0 copy-done.5
  434.1 2.1 subtract_convert_fusion
  436.2 0.0 all-gather.2.cloned.1.call-update
  436.2 0.0 all-reduce.5.cloned.1.call-start
  436.3 3.4 fusion
  439.6 13.8 %psum.23 = bf16[4,256,2]{1,2,0:T(2,128)(2,1)S(1)} all-reduce(bf16[4,256,2]{1,2,0:T(2,128)(2,1)S(1)} %fusion), channel_id=1, replica_groups=mesh['tok'=8,'lat'=16] {'tok'}, use_global_device_ids=true, to_apply=%region_9.10 | all-reduce | flops 2048 | bytes 8192 | tf_op jit(solution)/shard_map/psum | solution.py:73
  453.4 53.5 %all-gather.2.cloned.1.call-done = bf16[2048,2,1024]{2,0,1:T(8,128)(2,1)} async-done(((bf16[128,2,1024]{2,0,1:T(8,128)(2,1)}), bf16[2048,2,1024]{2,0,1:T(8,128)(2,1)}) %all-gather.2.cloned.1.call-update) | async-done | bytes 8388624 | tf_op jit(solution)/shard_map/all_gather | solution.py:63
  506.9 10.6 %gather_fusion.1 = bf16[32,128,2,1024]{3,1,2,0:T(8,128)(2,1)} fusion(bf16[16,128,2,1024]{3,1,0,2:T(8,128)(2,1)} %bitcast.60, s32[1024]{0:T(1024)S(1)} %pad_clamp_fusion), kind=kCustom, calls=%fused_computation.1 | custom fusion | bytes 33554560 | tf_op jit(solution)/shard_map/gather | solution.py:65
  517.5 12.8 %bitcast_convert_fusion.1 = bf16[4,8,128,256]{3,2,1,0:T(8,128)(2,1)} fusion(bf16[4,8,128,2,1024]{4,2,3,1,0:T(8,128)(2,1)} %bitcast.66, bf16[4,256,2,1024,1]{3,2,1,0,4:T(2,128)(2,1)} %bitcast.62), kind=kOutput, calls=%fused_computation.14 | convolution fusion | flops 4296015872 | bytes 23068672 | tf_op jit(solution)/shard_map/smrad,sjad->smrj/dot_general | solution.py:66
  530.3 0.0 all-reduce.5.cloned.1.call-update
  530.4 5.0 convert_reduce_fusion
  535.4 0.6 broadcast_multiply_fusion
  536.0 60.1 %all-reduce.5.cloned.1.call-done = bf16[4,8,128,256]{3,2,1,0:T(8,128)(2,1)} async-done(((bf16[4,8,128,256]{3,2,1,0:T(8,128)(2,1)}), bf16[4,8,128,256]{3,2,1,0:T(8,128)(2,1)}) %all-reduce.5.cloned.1.call-update) | async-done | bytes 2097168 | tf_op jit(solution)/shard_map/psum | solution.py:72
  596.2 0.0 copy-start.1
  596.2 5.1 convert_reduce_fusion.1
  601.2 0.0 copy-done.1
  601.2 10.7 %fusion.4 = bf16[4,256,2,1024]{3,1,2,0:T(8,128)(2,1)} fusion(f32[4,256,2]{1,2,0:T(2,128)S(1)} %get-tuple-element.22, f32[4,256]{1,0:T(4,128)S(1)} %broadcast_multiply_fusion.1, bf16[4,256,2,1024]{3,2,1,0:T(2,128)(2,1)S(1)} %copy-done.1, bf16[4,8,128,2,1024]{4,2,3,1,0:T(8,128)(2,1)} %bitcast.67, bf16[4,8,128,256]{3,2,1,0:T(8,128)(2,1)S(1)} %select_convert_fusion.1), kind=kOutput, calls=%fused_computation.11 | convolution fusion | flops 4307550208 | bytes 27275264 | tf_op jit(solution)/shard_map/smrj,smrad->sjad/dot_general | solution.py:83
  611.9 0.0 copy-start.2
  611.9 8.7 %copy.47 = bf16[4,256,2,1024]{3,2,1,0:T(2,128)(2,1)} copy(bf16[4,256,2,1024]{3,1,2,0:T(8,128)(2,1)} %fusion.4) | data formatting | bytes 8388608
  620.6 0.0 copy-done.2
  620.6 11.8 %bitcast_convert_fusion = bf16[4,2,1024,256]{3,2,1,0:T(8,128)(2,1)} fusion(bf16[4,8,128,2,1024]{4,2,3,1,0:T(8,128)(2,1)} %bitcast.65, bf16[4,8,128,256]{3,2,1,0:T(8,128)(2,1)S(1)} %copy-done.2, bf16[4,8,128,256]{3,2,1,0:T(8,128)(2,1)S(1)} %select_convert_fusion.1, f32[4,256]{1,0:T(4,128)S(1)} %broadcast_multiply_fusion.2), kind=kOutput, calls=%fused_computation.10 | convolution fusion | flops 4303355904 | bytes 25169920 | tf_op jit(solution)/shard_map/smrad,smrj->sadj/dot_general | solution.py:78
  (9 shorter events, 0.1 us)
Async XLA Ops:
  12.6 7.4 %copy-start.6 = (s32[16,16]{1,0:T(8,128)S(1)}, s32[16,16]{1,0:T(8,128)}, u32[]{:S(2)}) copy-start(s32[16,16]{1,0:T(8,128)} %param.11) | copy-start | bytes 3076
  12.6 131.3 %all-to-all-start = ((bf16[16,128,2,1024]{3,1,2,0:T(8,128)(2,1)}), bf16[16,128,2,1024]{3,1,2,0:T(8,128)(2,1)}, u32[]{:S(2)}, u32[]{:S(2)}) async-start(bf16[16,128,2,1024]{3,1,2,0:T(8,128)(2,1)} %stack.2), calls=%async_computation | async-start | bytes 16777216 | tf_op jit(solution)/shard_map/all_to_all | solution.py:37
  19.9 222.1 %all-reduce.3.cloned.1.call-start = ((), (), s32[]{:S(2)}) async-start(), calls=%async_computation.2 | async-start | bytes 8388608 | tf_op jit(solution)/shard_map/psum | solution.py:44
  168.0 74.0 %copy-start.4 = (f32[4,256]{1,0:T(4,128)S(1)}, f32[4,256]{1,0:T(4,128)}, u32[]{:S(2)}) copy-start(f32[4,256]{1,0:T(4,128)} %param.8) | copy-start | bytes 12292
  168.1 266.1 %reduce-scatter.2.cloned.1.call-start = ((), (), s32[]{:S(2)}) async-start(), calls=%async_computation.3 | async-start | bytes 8912896 | tf_op jit(solution)/shard_map/reduce_scatter | solution.py:57
  242.1 3.4 copy-start
  349.4 84.7 %copy-start.3 = (bf16[128,2,1024]{2,1,0:T(2,128)(2,1)S(1)}, bf16[128,2,1024]{2,1,0:T(2,128)(2,1)}, u32[]{:S(2)}) copy-start(bf16[128,2,1024]{2,1,0:T(2,128)(2,1)} %param.6) | copy-start | bytes 1572868
  349.4 84.7 %copy-start.5 = (f32[2,1024]{1,0:T(2,128)S(1)}, f32[2,1024]{1,0:T(2,128)}, u32[]{:S(2)}) copy-start(f32[2,1024]{1,0:T(2,128)} %param.10) | copy-start | bytes 24580
  349.4 157.5 %all-gather.2.cloned.1.call-start = ((), (), s32[]{:S(2)}) async-start(), calls=%async_computation.4 | async-start | bytes 8912896 | tf_op jit(solution)/shard_map/all_gather | solution.py:63
  436.2 160.0 %all-reduce.5.cloned.1.call-start = ((), (), s32[]{:S(2)}) async-start(), calls=%async_computation.5 | async-start | bytes 4194304 | tf_op jit(solution)/shard_map/psum | solution.py:72
  596.2 5.1 copy-start.1
  611.9 8.7 %copy-start.2 = (bf16[4,8,128,256]{3,2,1,0:T(8,128)(2,1)S(1)}, bf16[4,8,128,256]{3,2,1,0:T(8,128)(2,1)}, u32[]{:S(2)}) copy-start(bf16[4,8,128,256]{3,2,1,0:T(8,128)(2,1)} %all-reduce.5.cloned.1.call-done) | copy-start | bytes 6291460
Sparse Core Ops, SparseCore 0:
  168.2 73.8 all-reduce.2
  349.5 84.5 reduce-scatter.1
  436.8 69.9 all-gather.1
  530.5 65.6 all-reduce.4
